TPU v7x, 512 devices: a whole 4x8x8 slice. The times are simulated.
512 devices in a mesh: dp: 4 (over x), row: 16 (over y, core), col: 8 (over z).
Axes of the slice: x: 4, y: 8, z: 8, core: 2. Of those that a mesh axis runs over, the one named last changes fastest.
Arguments:
- grad_wi: bfloat16 [4, 4096, 16384], P('dp', 'row', 'col'), may hold values from -100 to 100
- grad_wo: bfloat16 [4, 16384, 4096], P('dp', 'row', 'col'), may hold values from -100 to 100
- row_wi: float32 [4096], P('row'), may hold values from 0.01 to 1
- col_wi: float32 [16384], P('col'), may hold values from 0.01 to 1
- row_wo: float32 [16384], P('row'), may hold values from 0.01 to 1
- col_wo: float32 [4096], P('col'), may hold values from 0.01 to 1
Outputs:
- update_wi: bfloat16 [4096, 16384], P('row', 'col')
- row_wi_new: float32 [4096], P('row')
- col_wi_new: float32 [16384], P('col')
- update_wo: bfloat16 [16384, 4096], P('row', 'col')
- row_wo_new: float32 [16384], P('row')
- col_wo_new: float32 [4096], P('col')
All inputs are finite; a program needn't handle non-finite values.
Results may differ from a plain program's by a relative error of at most 0.015.
Values may be sent and summed in bfloat16 or wider, within the bound.
A program may use at most 64 MiB of HBM per device.

v0:
```python
import jax
import jax.numpy as jnp
from jax import lax
from jax.sharding import PartitionSpec as P

D = 4096
FF = 16384
BETA = 0.8
EPS_SQUARE = 1e-30


def column_totals(square_wi, square_wo):
    return lax.psum((jnp.sum(square_wi, axis=0), jnp.sum(square_wo, axis=0)), "row")


def local(grad_wi, grad_wo, row_wi, col_wi, row_wo, col_wo):
    terms = (grad_wi[0].astype(jnp.float32), grad_wo[0].astype(jnp.float32))
    total_wi, total_wo = (
        lax.psum(terms[0].astype(jnp.bfloat16), "dp").astype(jnp.float32),
        lax.psum(terms[1].astype(jnp.bfloat16), "dp").astype(jnp.float32),
    )
    square_wi = total_wi * total_wi + EPS_SQUARE
    square_wo = total_wo * total_wo + EPS_SQUARE
    row_sum_wi, row_sum_wo = lax.psum(
        (jnp.sum(square_wi, axis=1), jnp.sum(square_wo, axis=1)), "col"
    )
    col_sum_wi, col_sum_wo = column_totals(square_wi, square_wo)
    row_new_wi = BETA * row_wi + (1.0 - BETA) * (row_sum_wi / FF)
    row_new_wo = BETA * row_wo + (1.0 - BETA) * (row_sum_wo / D)
    col_new_wi = BETA * col_wi + (1.0 - BETA) * (col_sum_wi / D)
    col_new_wo = BETA * col_wo + (1.0 - BETA) * (col_sum_wo / FF)
    raw_wi = total_wi / jnp.sqrt(row_new_wi[:, None] * col_new_wi[None, :])
    raw_wo = total_wo / jnp.sqrt(row_new_wo[:, None] * col_new_wo[None, :])
    local_squares = (jnp.sum(raw_wi * raw_wi), jnp.sum(raw_wo * raw_wo))
    energy_wi, energy_wo = lax.psum((local_squares[0], local_squares[1]), ("row", "col"))
    update_wi = (raw_wi / jnp.maximum(1.0, jnp.sqrt(energy_wi / (D * FF)))).astype(jnp.bfloat16)
    update_wo = (raw_wo / jnp.maximum(1.0, jnp.sqrt(energy_wo / (D * FF)))).astype(jnp.bfloat16)
    return (update_wi, row_new_wi, col_new_wi, update_wo, row_new_wo, col_new_wo)


def solution(mesh):
    return jax.shard_map(
        local,
        mesh=mesh,
        in_specs=(
            P("dp", "row", "col"),
            P("dp", "row", "col"),
            P("row"),
            P("col"),
            P("row"),
            P("col"),
        ),
        out_specs=(P("row", "col"), P("row"), P("col"), P("row", "col"), P("row"), P("col")),
        check_vma=False,
    )
```

profile of v0, /device:TPU:64, one launch (start us, length us, event | category | flops | bytes accessed | tf_op | source)
XLA Modules:
  0.0 412.7 jit_solution(8415651941492895730)
XLA Ops:
  7.2 0.0 all-reduce.6.cloned.1.call-start
  7.2 0.7 all-reduce.6.cloned.1.call-update
  7.9 76.1 %all-reduce.6.cloned.1.call-done = (bf16[256,2048]{1,0:T(8,128)(2,1)}, bf16[1024,512]{1,0:T(8,128)(2,1)}) async-done(((bf16[256,2048]{1,0:T(8,128)(2,1)}, bf16[1024,512]{1,0:T(8,128)(2,1)}), (bf16[256,2048]{1,0:T(8,128)(2,1)}, bf16[1024,512]{1,0:T(8,128)(2,1)})) %all-reduce.6.cloned.1.call-update) | async-done | bytes 2097168 | tf_op jit(solution)/shard_map/psum | solution.py:19
  84.0 0.0 copy-start.1
  84.0 0.0 copy-start.9
  84.0 0.0 copy-start.7
  84.0 0.0 copy-start.6
  84.0 1.8 fusion.5
  85.8 0.0 copy-done.1
  85.8 0.0 copy-start.8
  85.8 0.0 copy-start
  85.8 0.5 fusion.2
  86.3 16.8 %all-reduce.2 = (f32[256]{0:T(256)S(1)}, f32[1024]{0:T(1024)S(1)}) all-reduce(f32[256]{0:T(256)S(1)} %get-tuple-element.8, f32[1024]{0:T(1024)S(1)} %get-tuple-element.6), channel_id=1, replica_groups=mesh['dp'=4,'row'=16,'col'=8] {'col'}, use_global_device_ids=true, to_apply=%region_2.0 | all-reduce | flops 1280 | bytes 10240 | tf_op jit(solution)/shard_map/psum | solution.py:24
  103.1 0.0 copy-done.9
  103.1 0.0 copy-start.5
  103.1 0.0 copy-done.7
  103.1 0.0 copy-start.3
  103.2 45.7 %all-reduce.1 = (f32[2048]{0:T(1024)S(1)}, f32[512]{0:T(512)S(1)}) all-reduce(f32[2048]{0:T(1024)S(1)} %get-tuple-element.9, f32[512]{0:T(512)S(1)} %get-tuple-element.7), channel_id=1, replica_groups=mesh['dp'=4,'row'=16,'col'=8] {'row'}, use_global_device_ids=true, to_apply=%region_4.0 | all-reduce | flops 2560 | bytes 20480 | tf_op jit(solution)/shard_map/psum | solution.py:13
  148.9 0.0 copy-done.6
  148.9 0.0 copy-start.2
  148.9 1.5 multiply_reduce_fusion.1
  150.4 0.0 copy-done.8
  150.4 0.0 copy-done
  150.4 0.0 copy-start.4
  150.4 1.4 multiply_reduce_fusion
  151.9 249.7 %all-reduce = (f32[]{:T(128)}, f32[]{:T(128)}) all-reduce(f32[]{:T(128)} %multiply_reduce_fusion.1, f32[]{:T(128)} %multiply_reduce_fusion), channel_id=1, replica_groups=mesh['dp'=4,'row'=16,'col'=8] {'row','col'}, use_global_device_ids=true, to_apply=%region_6.0 | all-reduce | flops 2 | bytes 16 | tf_op jit(solution)/shard_map/psum | solution.py:35
  403.0 0.0 copy-done.5
  403.0 0.0 copy-done.2
  403.0 1.4 divide_convert_fusion.1
  404.4 0.0 copy-done.3
  404.4 0.0 copy-done.4
  404.4 1.4 divide_convert_fusion
  (4 shorter events, 0.0 us)
Async XLA Ops:
  7.2 76.8 %all-reduce.6.cloned.1.call-start = ((), (), s32[]{:S(2)}) async-start(), calls=%async_computation | async-start | bytes 4194304 | tf_op jit(solution)/shard_map/psum | solution.py:19
  84.0 1.8 copy-start.1
  84.0 19.1 %copy-start.9 = (f32[256]{0:T(256)S(1)}, f32[256]{0:T(256)}, u32[]{:S(2)}) copy-start(f32[256]{0:T(256)} %param.8) | copy-start | bytes 3076
  84.0 19.1 %copy-start.7 = (f32[1024]{0:T(1024)S(1)}, f32[1024]{0:T(1024)}, u32[]{:S(2)}) copy-start(f32[1024]{0:T(1024)} %param.10) | copy-start | bytes 12292
  84.0 64.9 %copy-start.6 = (f32[2048]{0:T(1024)S(1)}, f32[2048]{0:T(1024)}, u32[]{:S(2)}) copy-start(f32[2048]{0:T(1024)} %param.9) | copy-start | bytes 24580
  85.8 64.6 %copy-start.8 = (f32[512]{0:T(512)S(1)}, f32[512]{0:T(512)}, u32[]{:S(2)}) copy-start(f32[512]{0:T(512)} %param.11) | copy-start | bytes 6148
  85.8 64.6 %copy-start = (bf16[1024,512]{1,0:T(8,128)(2,1)S(1)}, bf16[1024,512]{1,0:T(8,128)(2,1)}, u32[]{:S(2)}) copy-start(bf16[1024,512]{1,0:T(8,128)(2,1)} %get-tuple-element.17) | copy-start | bytes 3145732
  103.1 299.9 %copy-start.5 = (f32[256]{0:T(256)}, f32[256]{0:T(256)S(1)}, u32[]{:S(2)}) copy-start(f32[256]{0:T(256)S(1)} %multiply_add_fusion.3) | copy-start | bytes 3076
  103.1 301.3 %copy-start.3 = (f32[1024]{0:T(1024)}, f32[1024]{0:T(1024)S(1)}, u32[]{:S(2)}) copy-start(f32[1024]{0:T(1024)S(1)} %multiply_add_fusion.1) | copy-start | bytes 12292
  148.9 254.1 %copy-start.2 = (f32[2048]{0:T(1024)}, f32[2048]{0:T(1024)S(1)}, u32[]{:S(2)}) copy-start(f32[2048]{0:T(1024)S(1)} %multiply_add_fusion) | copy-start | bytes 24580
  150.4 254.0 %copy-start.4 = (f32[512]{0:T(512)}, f32[512]{0:T(512)S(1)}, u32[]{:S(2)}) copy-start(f32[512]{0:T(512)S(1)} %multiply_add_fusion.2) | copy-start | bytes 6148
Sparse Core Ops, SparseCore 0:
  10.4 73.4 all-reduce.5
where the time goes:
time: 413 us
  blocking collectives  312 us (76%)
  waiting for transfers between devices  76.8 us (19%)
  between operations  15.5 us (4%)
  other arithmetic  8.11 us (2%)
    psum x1, blocking collectives, local(): lax.psum((local_squares[0], local_squares[1]), ('row', 'col'))  250 us
    psum x1, waiting for transfers between devices, local(): lax.psum(terms[0].astype(jnp.bfloat16), 'dp').astype(jnp.float32)  76.1 us
    psum x1, blocking collectives, column_totals(): lax.psum((jnp.sum(square_wi, axis=0), jnp.sum(square_wo, axis=0)), 'row')  45.7 us
    psum x1, blocking collectives, local(): lax.psum((jnp.sum(square_wi, axis=1), jnp.sum(square_wo, axis=1)), 'col')  16.8 us
  transfers between devices with their start and end apart: 1, of which 1 were waited for; matrix products, arithmetic and copies ran while one was open for 0% of the time, Pallas kernels for 0%

commit v1 on v0

--- a/solution.py
+++ b/solution.py
@@ -32,7 +32,7 @@
     raw_wi = total_wi / jnp.sqrt(row_new_wi[:, None] * col_new_wi[None, :])
     raw_wo = total_wo / jnp.sqrt(row_new_wo[:, None] * col_new_wo[None, :])
     local_squares = (jnp.sum(raw_wi * raw_wi), jnp.sum(raw_wo * raw_wo))
-    energy_wi, energy_wo = lax.psum((local_squares[0], local_squares[1]), ("row", "col"))
+    energy_wi, energy_wo = lax.psum(lax.psum((local_squares[0], local_squares[1]), "row"), "col")
     update_wi = (raw_wi / jnp.maximum(1.0, jnp.sqrt(energy_wi / (D * FF)))).astype(jnp.bfloat16)
     update_wo = (raw_wo / jnp.maximum(1.0, jnp.sqrt(energy_wo / (D * FF)))).astype(jnp.bfloat16)
     return (update_wi, row_new_wi, col_new_wi, update_wo, row_new_wo, col_new_wo)

time: 413 us -> 205 us (0.50)
  the two profiles are of different devices: /device:TPU:64 before, /device:TPU:32 now
where the time goes in v1:
time: 205 us
  blocking collectives  104 us (51%)
  waiting for transfers between devices  77.1 us (38%)
  between operations  15.5 us (8%)
  other arithmetic  8.11 us (4%)
    psum x1, waiting for transfers between devices, local(): lax.psum(terms[0].astype(jnp.bfloat16), 'dp').astype(jnp.float32)  76.4 us
    psum x1, blocking collectives, column_totals(): lax.psum((jnp.sum(square_wi, axis=0), jnp.sum(square_wo, axis=0)), 'row')  45.8 us
    psum x1, blocking collectives, local(): lax.psum((local_squares[0], local_squares[1]), 'row')  24.2 us
    psum x1, blocking collectives, local(): lax.psum((jnp.sum(square_wi, axis=1), jnp.sum(square_wo, axis=1)), 'col')  18.4 us
    psum x1, blocking collectives, local(): lax.psum(lax.psum((local_squares[0], local_squares[1]), 'row'), 'col')  15.3 us
  transfers between devices with their start and end apart: 1, of which 1 were waited for; matrix products, arithmetic and copies ran while one was open for 0% of the time, Pallas kernels for 0%

profile of v1, /device:TPU:32, one launch (start us, length us, event | category | flops | bytes accessed | tf_op | source)
XLA Modules:
  0.0 204.5 jit_solution(1561780827785561097)
XLA Ops:
  7.2 0.0 all-reduce.7.cloned.1.call-start
  7.2 0.7 all-reduce.7.cloned.1.call-update
  7.9 76.4 %all-reduce.7.cloned.1.call-done = (bf16[256,2048]{1,0:T(8,128)(2,1)}, bf16[1024,512]{1,0:T(8,128)(2,1)}) async-done(((bf16[256,2048]{1,0:T(8,128)(2,1)}, bf16[1024,512]{1,0:T(8,128)(2,1)}), (bf16[256,2048]{1,0:T(8,128)(2,1)}, bf16[1024,512]{1,0:T(8,128)(2,1)})) %all-reduce.7.cloned.1.call-update) | async-done | bytes 2097168 | tf_op jit(solution)/shard_map/psum | solution.py:19
  84.3 0.0 copy-start.1
  84.3 0.0 copy-start.9
  84.4 0.0 copy-start.7
  84.4 0.0 copy-start.6
  84.4 1.8 fusion.5
  86.1 0.0 copy-done.1
  86.1 0.0 copy-start.8
  86.2 0.0 copy-start
  86.2 0.5 fusion.2
  86.7 18.4 %all-reduce.3 = (f32[256]{0:T(256)S(1)}, f32[1024]{0:T(1024)S(1)}) all-reduce(f32[256]{0:T(256)S(1)} %get-tuple-element.8, f32[1024]{0:T(1024)S(1)} %get-tuple-element.6), channel_id=1, replica_groups=mesh['dp'=4,'row'=16,'col'=8] {'col'}, use_global_device_ids=true, to_apply=%region_2.0 | all-reduce | flops 1280 | bytes 10240 | tf_op jit(solution)/shard_map/psum | solution.py:24
  105.1 0.0 copy-done.9
  105.1 0.0 copy-start.5
  105.1 0.0 copy-done.7
  105.2 0.0 copy-start.3
  105.2 45.8 %all-reduce.1 = (f32[2048]{0:T(1024)S(1)}, f32[512]{0:T(512)S(1)}) all-reduce(f32[2048]{0:T(1024)S(1)} %get-tuple-element.9, f32[512]{0:T(512)S(1)} %get-tuple-element.7), channel_id=1, replica_groups=mesh['dp'=4,'row'=16,'col'=8] {'row'}, use_global_device_ids=true, to_apply=%region_4.0 | all-reduce | flops 2560 | bytes 20480 | tf_op jit(solution)/shard_map/psum | solution.py:13
  150.9 0.0 copy-done.6
  150.9 0.0 copy-start.2
  150.9 1.5 multiply_reduce_fusion.1
  152.5 0.0 copy-done.8
  152.5 0.0 copy-done
  152.5 0.0 copy-start.4
  152.5 1.4 multiply_reduce_fusion
  153.9 24.2 %all-reduce = (f32[]{:T(128)}, f32[]{:T(128)}) all-reduce(f32[]{:T(128)} %multiply_reduce_fusion.1, f32[]{:T(128)} %multiply_reduce_fusion), channel_id=1, replica_groups=mesh['dp'=4,'row'=16,'col'=8] {'row'}, use_global_device_ids=true, to_apply=%region_6.0 | all-reduce | flops 2 | bytes 16 | tf_op jit(solution)/shard_map/psum | solution.py:35
  178.1 15.3 %all-reduce.2 = (f32[]{:T(128)}, f32[]{:T(128)}) all-reduce(f32[]{:T(128)} %get-tuple-element.10, f32[]{:T(128)} %get-tuple-element.11), channel_id=1, replica_groups=mesh['dp'=4,'row'=16,'col'=8] {'col'}, use_global_device_ids=true, to_apply=%region_7.0 | all-reduce | flops 2 | bytes 16 | tf_op jit(solution)/shard_map/psum | solution.py:35
  194.8 0.0 copy-done.5
  194.8 0.0 copy-done.2
  194.8 1.4 divide_convert_fusion.1
  196.2 0.0 copy-done.3
  196.2 0.0 copy-done.4
  196.2 1.4 divide_convert_fusion
  (4 shorter events, 0.0 us)
Async XLA Ops:
  7.2 77.2 %all-reduce.7.cloned.1.call-start = ((), (), s32[]{:S(2)}) async-start(), calls=%async_computation | async-start | bytes 4194304 | tf_op jit(solution)/shard_map/psum | solution.py:19
  84.3 1.8 copy-start.1
  84.3 20.7 %copy-start.9 = (f32[256]{0:T(256)S(1)}, f32[256]{0:T(256)}, u32[]{:S(2)}) copy-start(f32[256]{0:T(256)} %param.8) | copy-start | bytes 3076
  84.4 20.8 %copy-start.7 = (f32[1024]{0:T(1024)S(1)}, f32[1024]{0:T(1024)}, u32[]{:S(2)}) copy-start(f32[1024]{0:T(1024)} %param.10) | copy-start | bytes 12292
  84.4 66.6 %copy-start.6 = (f32[2048]{0:T(1024)S(1)}, f32[2048]{0:T(1024)}, u32[]{:S(2)}) copy-start(f32[2048]{0:T(1024)} %param.9) | copy-start | bytes 24580
  86.1 66.3 %copy-start.8 = (f32[512]{0:T(512)S(1)}, f32[512]{0:T(512)}, u32[]{:S(2)}) copy-start(f32[512]{0:T(512)} %param.11) | copy-start | bytes 6148
  86.2 66.3 %copy-start = (bf16[1024,512]{1,0:T(8,128)(2,1)S(1)}, bf16[1024,512]{1,0:T(8,128)(2,1)}, u32[]{:S(2)}) copy-start(bf16[1024,512]{1,0:T(8,128)(2,1)} %get-tuple-element.19) | copy-start | bytes 3145732
  105.1 89.7 %copy-start.5 = (f32[256]{0:T(256)}, f32[256]{0:T(256)S(1)}, u32[]{:S(2)}) copy-start(f32[256]{0:T(256)S(1)} %multiply_add_fusion.3) | copy-start | bytes 3076
  105.2 91.1 %copy-start.3 = (f32[1024]{0:T(1024)}, f32[1024]{0:T(1024)S(1)}, u32[]{:S(2)}) copy-start(f32[1024]{0:T(1024)S(1)} %multiply_add_fusion.1) | copy-start | bytes 12292
  150.9 43.9 %copy-start.2 = (f32[2048]{0:T(1024)}, f32[2048]{0:T(1024)S(1)}, u32[]{:S(2)}) copy-start(f32[2048]{0:T(1024)S(1)} %multiply_add_fusion) | copy-start | bytes 24580
  152.5 43.8 %copy-start.4 = (f32[512]{0:T(512)}, f32[512]{0:T(512)S(1)}, u32[]{:S(2)}) copy-start(f32[512]{0:T(512)S(1)} %multiply_add_fusion.2) | copy-start | bytes 6148
Sparse Core Ops, SparseCore 0:
  10.4 73.8 all-reduce.6
